TPU v7x, 32 devices: a whole 2x2x4 slice. The times are simulated.
32 devices in a mesh: replica: 4 (over x, core), shard: 8 (over z, y).
Axes of the slice: x: 2, y: 2, z: 4, core: 2. Of those that a mesh axis runs over, the one named last changes fastest.
Arguments:
- tokens: bfloat16 [32768, 768], P(('replica', 'shard')), may hold values from -6 to 6
- gain_attn: bfloat16 [768], P('shard'), may hold values from 0.099609375 to 1.8984375
- w_qkv: bfloat16 [768, 2304], P('shard'), may hold values from -0.3125 to 0.3125
- w_out: bfloat16 [768, 768], P('shard'), may hold values from -0.875 to 0.875
- gain_ffn: bfloat16 [768], P('shard'), may hold values from 0.099609375 to 1.8984375
- w_in: bfloat16 [768, 2304], P('shard'), may hold values from -0.21875 to 0.21875
- w_down: bfloat16 [1152, 768], P('shard'), may hold values from -0.1875 to 0.1875
- cotangent: bfloat16 [32768, 768], P(('replica', 'shard')), may hold values from -6 to 6
Outputs:
- output: bfloat16 [32768, 768], P(('replica', 'shard'))
- input_grad: bfloat16 [32768, 768], P(('replica', 'shard'))
- grad_gain_attn: float32 [768], P('shard')
- grad_qkv: float32 [768, 2304], P('shard')
- grad_out: float32 [768, 768], P('shard')
- grad_gain_ffn: float32 [768], P('shard')
- grad_in: float32 [768, 2304], P('shard')
- grad_down: float32 [1152, 768], P('shard')
All inputs are finite; a program needn't handle non-finite values.
Results may differ from a plain program's by a relative error of at most 0.018.
Values may be sent and summed in bfloat16 or wider, within the bound.
A program may use at most 128 MiB of HBM per device.

v0:
```python
import math
import jax
import jax.numpy as jnp
from jax import lax
from jax.sharding import PartitionSpec as P

D = 768
HEADS = 12
HEAD_DIM = 64
FF = 1152
WINDOW = 128
LENGTH = 1024
epsilon = 1e-05


def normalize(values):
    centre = values - jnp.mean(values, axis=-1, keepdims=True)
    inverse = lax.rsqrt(jnp.mean(centre * centre, axis=-1, keepdims=True) + epsilon)
    return (centre * inverse, inverse)


def norm_back(grad_norm, standard, inverse, gain):
    scaled = grad_norm * gain
    return inverse * (
        scaled
        - jnp.mean(scaled, axis=-1, keepdims=True)
        - standard * jnp.mean(scaled * standard, axis=-1, keepdims=True)
    )


def rotary_tables(count):
    half_dim = HEAD_DIM // 2
    freqs = 10000.0 ** (-(jnp.arange(half_dim, dtype=jnp.float32) * 2.0) / HEAD_DIM)
    places = (jnp.arange(count, dtype=jnp.int32) % LENGTH).astype(jnp.float32)
    angles = places[:, None] * freqs[None, :]
    angles = jnp.concatenate([angles, angles], axis=1)
    return (jnp.cos(angles)[:, None, :], jnp.sin(angles)[:, None, :])


def rotate_half(values):
    half_dim = values.shape[-1] // 2
    return jnp.concatenate([-values[..., half_dim:], values[..., :half_dim]], axis=-1)


def rotate_back(values):
    half_dim = values.shape[-1] // 2
    return jnp.concatenate([values[..., half_dim:], -values[..., :half_dim]], axis=-1)


def windows(field, block_rows, margin):
    seq_count = field.shape[0] // LENGTH
    blocks = LENGTH // block_rows
    shaped = field.reshape(seq_count, LENGTH, HEADS, HEAD_DIM)
    padded = jnp.pad(shaped, ((0, 0), (margin, block_rows - margin), (0, 0), (0, 0)))
    first = padded[:, :LENGTH].reshape(seq_count, blocks, block_rows, HEADS, HEAD_DIM)
    second = padded[:, block_rows : block_rows + LENGTH].reshape(
        seq_count, blocks, block_rows, HEADS, HEAD_DIM
    )
    joined = jnp.concatenate([first, second[:, :, : 2 * margin]], axis=2)
    return joined.reshape(seq_count * blocks, block_rows + 2 * margin, HEADS, HEAD_DIM)


def unwindow(field, block_rows, margin):
    blocks = LENGTH // block_rows
    seq_count = field.shape[0] // blocks
    shaped = field.reshape(seq_count, blocks, block_rows + 2 * margin, HEADS, HEAD_DIM)
    first = shaped[:, :, :block_rows].reshape(seq_count, LENGTH, HEADS, HEAD_DIM)
    second = jnp.pad(
        shaped[:, :, block_rows:], ((0, 0), (0, 0), (0, block_rows - 2 * margin), (0, 0), (0, 0))
    )
    second = second.reshape(seq_count, LENGTH, HEADS, HEAD_DIM)
    whole = jnp.pad(first, ((0, 0), (0, block_rows), (0, 0), (0, 0))) + jnp.pad(
        second, ((0, 0), (block_rows, 0), (0, 0), (0, 0))
    )
    return whole[:, margin : margin + LENGTH].reshape(seq_count * LENGTH, HEADS, HEAD_DIM)


def to_items(field):
    per_group = math.gcd(HEADS, 4)
    head_groups = HEADS // per_group
    count, rows = (field.shape[0], field.shape[1])
    shaped = field.reshape(count, rows, head_groups, per_group, HEAD_DIM).transpose(0, 2, 1, 3, 4)
    return shaped.reshape(count * head_groups, rows, per_group, HEAD_DIM)


def from_items(field):
    per_group = math.gcd(HEADS, 4)
    head_groups = HEADS // per_group
    count, rows = (field.shape[0] // head_groups, field.shape[1])
    shaped = field.reshape(count, head_groups, rows, per_group, HEAD_DIM).transpose(0, 2, 1, 3, 4)
    return shaped.reshape(count, rows, HEADS, HEAD_DIM)


def block_scores(query_part, key_part, start, block_rows, margin):
    span = key_part.shape[0]
    query_pos = start + jnp.arange(block_rows, dtype=jnp.int32)[:, None]
    key_pos = start - margin + jnp.arange(span, dtype=jnp.int32)[None, :]
    allowed = (key_pos >= 0) & (key_pos < LENGTH) & (jnp.abs(query_pos - key_pos) <= margin)
    raw = jnp.einsum(
        "qhd,khd->hqk", query_part, key_part, preferred_element_type=jnp.float32
    ) * HEAD_DIM ** (-0.5)
    return jnp.where(allowed[None], raw, -1e30)


def block_starts(count, block_rows):
    per_group = math.gcd(HEADS, 4)
    blocks = LENGTH // block_rows
    starts = jnp.arange(count, dtype=jnp.int32) % blocks * block_rows
    return jnp.repeat(starts, HEADS // per_group)


def attend_forward(queries, keys, values):
    count_tok = queries.shape[0]
    block_rows = min(512, LENGTH)
    margin = WINDOW // 2
    query_items = to_items(queries.reshape(count_tok // block_rows, block_rows, HEADS, HEAD_DIM))
    key_items = to_items(windows(keys, block_rows, margin))
    value_items = to_items(windows(values, block_rows, margin))
    starts = block_starts(count_tok // block_rows, block_rows)

    def one_block(pieces):
        query_part, key_part, value_part, start = pieces
        scores = block_scores(query_part, key_part, start, block_rows, margin)
        top = jnp.max(scores, axis=-1, keepdims=True)
        expo = jnp.exp(scores - top)
        total = jnp.sum(expo, axis=-1, keepdims=True)
        probs = (expo / total).astype(jnp.bfloat16)
        mixed = jnp.einsum("hqk,khd->qhd", probs, value_part, preferred_element_type=jnp.float32)
        return (mixed.astype(jnp.bfloat16), top[..., 0] + jnp.log(total[..., 0]))

    mixed, log_totals = lax.map(one_block, (query_items, key_items, value_items, starts))
    return (from_items(mixed).reshape(count_tok, D), log_totals)


def attend_backward(queries, keys, values, grad_mixed, log_totals):
    count_tok = queries.shape[0]
    block_rows = min(512, LENGTH)
    margin = WINDOW // 2
    scale = HEAD_DIM ** (-0.5)
    query_items = to_items(queries.reshape(count_tok // block_rows, block_rows, HEADS, HEAD_DIM))
    grad_items = to_items(grad_mixed.reshape(count_tok // block_rows, block_rows, HEADS, HEAD_DIM))
    key_items = to_items(windows(keys, block_rows, margin))
    value_items = to_items(windows(values, block_rows, margin))
    starts = block_starts(count_tok // block_rows, block_rows)

    def one_block(pieces):
        query_part, key_part, value_part, grad_part, log_part, start = pieces
        scores = block_scores(query_part, key_part, start, block_rows, margin)
        probs = jnp.exp(scores - log_part[..., None])
        grad_probs = jnp.einsum(
            "qhd,khd->hqk", grad_part, value_part, preferred_element_type=jnp.float32
        )
        centre = jnp.sum(grad_probs * probs, axis=-1, keepdims=True)
        grad_scores = (probs * (grad_probs - centre)).astype(jnp.bfloat16)
        grad_query = (
            jnp.einsum("hqk,khd->qhd", grad_scores, key_part, preferred_element_type=jnp.float32)
            * scale
        )
        grad_key = (
            jnp.einsum("hqk,qhd->khd", grad_scores, query_part, preferred_element_type=jnp.float32)
            * scale
        )
        grad_value = jnp.einsum(
            "hqk,qhd->khd",
            probs.astype(jnp.bfloat16),
            grad_part,
            preferred_element_type=jnp.float32,
        )
        return (grad_query, grad_key, grad_value)

    grad_query, grad_key, grad_value = lax.map(
        one_block, (query_items, key_items, value_items, grad_items, log_totals, starts)
    )
    grad_query = from_items(grad_query).reshape(count_tok, HEADS, HEAD_DIM)
    grad_key = unwindow(from_items(grad_key), block_rows, margin)
    grad_value = unwindow(from_items(grad_value), block_rows, margin)
    return (grad_query, grad_key, grad_value)


def body(tokens, gain_attn, w_qkv, w_out, gain_ffn, w_in, w_down, cotangent):
    count_tok = tokens.shape[0]
    gain_one, joint_weight, out_weight = (
        lax.all_gather(gain_attn, "shard", axis=0, tiled=True),
        lax.all_gather(w_qkv, "shard", axis=0, tiled=True),
        lax.all_gather(w_out, "shard", axis=0, tiled=True),
    )
    gain_two, in_weight, down_weight = (
        lax.all_gather(gain_ffn, "shard", axis=0, tiled=True),
        lax.all_gather(w_in, "shard", axis=0, tiled=True),
        lax.all_gather(w_down, "shard", axis=0, tiled=True),
    )
    stream = tokens.astype(jnp.float32)
    standard_one, inverse_one = normalize(stream)
    normed_attn = (standard_one * gain_one.astype(jnp.float32)).astype(jnp.bfloat16)
    projected = jnp.dot(normed_attn, joint_weight, preferred_element_type=jnp.float32)
    projected = projected.reshape(count_tok, 3, HEADS, HEAD_DIM)
    cosine, sine = rotary_tables(count_tok)
    raw_query = projected[:, 0]
    raw_key = projected[:, 1]
    queries = (raw_query * cosine + rotate_half(raw_query) * sine).astype(jnp.bfloat16)
    keys = (raw_key * cosine + rotate_half(raw_key) * sine).astype(jnp.bfloat16)
    values = projected[:, 2].astype(jnp.bfloat16)
    attended, log_totals = attend_forward(queries, keys, values)
    after_attn = stream + jnp.dot(attended, out_weight, preferred_element_type=jnp.float32)
    standard_two, inverse_two = normalize(after_attn)
    normed_ffn = (standard_two * gain_two.astype(jnp.float32)).astype(jnp.bfloat16)
    gate_up = jnp.dot(normed_ffn, in_weight, preferred_element_type=jnp.float32)
    lifted = gate_up[:, :FF]
    gate_part = gate_up[:, FF:]
    normal_cdf = 0.5 * (1.0 + lax.erf(lifted * 0.7071067811865476))
    gelu_value = lifted * normal_cdf
    activated = (gelu_value * gate_part).astype(jnp.bfloat16)
    final = after_attn + jnp.dot(activated, down_weight, preferred_element_type=jnp.float32)
    output = final.astype(jnp.bfloat16)
    gain_one, joint_weight, out_weight = (
        lax.all_gather(gain_attn, "shard", axis=0, tiled=True),
        lax.all_gather(w_qkv, "shard", axis=0, tiled=True),
        lax.all_gather(w_out, "shard", axis=0, tiled=True),
    )
    gain_two, in_weight, down_weight = (
        lax.all_gather(gain_ffn, "shard", axis=0, tiled=True),
        lax.all_gather(w_in, "shard", axis=0, tiled=True),
        lax.all_gather(w_down, "shard", axis=0, tiled=True),
    )
    grad_final = cotangent.astype(jnp.float32)
    grad_down = jnp.einsum("tf,td->fd", activated, cotangent, preferred_element_type=jnp.float32)
    grad_act = jnp.einsum("td,fd->tf", cotangent, down_weight, preferred_element_type=jnp.float32)
    density = jnp.exp(-0.5 * lifted * lifted) * 0.3989422804014327
    grad_lifted = grad_act * gate_part * (normal_cdf + lifted * density)
    grad_gate = grad_act * gelu_value
    grad_gate_up = jnp.concatenate([grad_lifted, grad_gate], axis=1).astype(jnp.bfloat16)
    grad_in = jnp.einsum("td,te->de", normed_ffn, grad_gate_up, preferred_element_type=jnp.float32)
    grad_norm_ffn = jnp.einsum(
        "te,de->td", grad_gate_up, in_weight, preferred_element_type=jnp.float32
    )
    grad_gain_ffn = jnp.sum(grad_norm_ffn * standard_two, axis=0)
    grad_after = grad_final + norm_back(
        grad_norm_ffn, standard_two, inverse_two, gain_two.astype(jnp.float32)
    )
    ffn_members = (grad_gain_ffn, grad_in, grad_down)
    owned_gain_ffn, owned_in, owned_down = (
        lax.psum_scatter(ffn_members[0], "shard", scatter_dimension=0, tiled=True),
        lax.psum_scatter(ffn_members[1], "shard", scatter_dimension=0, tiled=True),
        lax.psum_scatter(ffn_members[2], "shard", scatter_dimension=0, tiled=True),
    )
    grad_branch = grad_after.astype(jnp.bfloat16)
    grad_out = jnp.einsum("td,te->de", attended, grad_branch, preferred_element_type=jnp.float32)
    grad_attended = jnp.einsum(
        "te,de->td", grad_branch, out_weight, preferred_element_type=jnp.float32
    ).astype(jnp.bfloat16)
    grad_query, grad_key, grad_value = attend_backward(
        queries, keys, values, grad_attended, log_totals
    )
    grad_query = grad_query * cosine + rotate_back(grad_query * sine)
    grad_key = grad_key * cosine + rotate_back(grad_key * sine)
    grad_projected = jnp.stack([grad_query, grad_key, grad_value], axis=1)
    grad_projected = grad_projected.reshape(count_tok, 3 * D).astype(jnp.bfloat16)
    grad_qkv = jnp.einsum(
        "td,te->de", normed_attn, grad_projected, preferred_element_type=jnp.float32
    )
    grad_norm_attn = jnp.einsum(
        "te,de->td", grad_projected, joint_weight, preferred_element_type=jnp.float32
    )
    grad_gain_attn = jnp.sum(grad_norm_attn * standard_one, axis=0)
    input_grad = grad_after + norm_back(
        grad_norm_attn, standard_one, inverse_one, gain_one.astype(jnp.float32)
    )
    attn_members = (grad_gain_attn, grad_qkv, grad_out)
    owned_gain_attn, owned_qkv, owned_out = (
        lax.psum_scatter(attn_members[0], "shard", scatter_dimension=0, tiled=True),
        lax.psum_scatter(attn_members[1], "shard", scatter_dimension=0, tiled=True),
        lax.psum_scatter(attn_members[2], "shard", scatter_dimension=0, tiled=True),
    )
    summed = (
        lax.psum(owned_gain_attn.astype(jnp.bfloat16), "replica").astype(jnp.float32),
        lax.psum(owned_qkv.astype(jnp.bfloat16), "replica").astype(jnp.float32),
        lax.psum(owned_out.astype(jnp.bfloat16), "replica").astype(jnp.float32),
        lax.psum(owned_gain_ffn.astype(jnp.bfloat16), "replica").astype(jnp.float32),
        lax.psum(owned_in.astype(jnp.bfloat16), "replica").astype(jnp.float32),
        lax.psum(owned_down.astype(jnp.bfloat16), "replica").astype(jnp.float32),
    )
    return (
        output,
        input_grad.astype(jnp.bfloat16),
        summed[0],
        summed[1],
        summed[2],
        summed[3],
        summed[4],
        summed[5],
    )


def solution(mesh):
    return jax.shard_map(
        body,
        mesh=mesh,
        in_specs=(
            P(("replica", "shard"), None),
            P("shard"),
            P("shard", None),
            P("shard", None),
            P("shard"),
            P("shard", None),
            P("shard", None),
            P(("replica", "shard"), None),
        ),
        out_specs=(
            P(("replica", "shard"), None),
            P(("replica", "shard"), None),
            P("shard"),
            P("shard", None),
            P("shard", None),
            P("shard"),
            P("shard", None),
            P("shard", None),
        ),
        check_vma=False,
    )
```

profile of v0, /device:TPU:0, one launch (start us, length us, event | category | flops | bytes accessed | tf_op | source)
XLA Modules:
  0.0 722.2 jit_solution(9472683614992483625)
XLA Ops:
  14.4 23.5 %all-reduce.13 = (bf16[768]{0:T(1024)(128)(2,1)S(1)}, bf16[768]{0:T(1024)(128)(2,1)S(1)}) all-reduce(bf16[768]{0:T(1024)(128)(2,1)S(1)} %dynamic-update-slice, bf16[768]{0:T(1024)(128)(2,1)S(1)} %dynamic-update-slice.1), channel_id=1, replica_groups=mesh['replica'=4,'shard'=8] {'shard'}, use_global_device_ids=true, to_apply=%add.8 | all-reduce | flops 1536 | bytes 6144
  39.1 4.4 fusion.101
  46.5 31.9 %all-gather.5.cloned.1.call-done = bf16[768,2304]{1,0:T(8,128)(2,1)} async-done(((bf16[96,2304]{1,0:T(8,128)(2,1)}), bf16[768,2304]{1,0:T(8,128)(2,1)}) %all-gather.5.cloned.1.call-update) | async-done | bytes 3538960 | tf_op jit(solution)/shard_map/all_gather | solution.py:184
  78.4 6.0 fusion.96
  84.4 4.2 slice_bitcast_fusion
  112.8 5.6 squeeze.70
  118.4 4.7 fusion.90
  133.8 4.4 concatenate.87
  143.6 61.0 %while.30 = (s32[]{:T(128)}, bf16[6,512,4,64]{1,3,2,0:T(8,128)(2,1)}, f32[6,4,512]{2,1,0:T(4,128)}, bf16[6,640,4,64]{1,3,2,0:T(8,128)(2,1)}, s32[6]{0:T(128)S(1)...) while((s32[]{:T(128)}, ...), condition=%wide.region_5.6_spmd, body=%wide.region_2.5_spmd.sunk | while | flops 352716416 | bytes 18297728 | solution.py:131
  214.7 10.7 %fusion.110 = f32[1024,2304]{1,0:T(8,128)} fusion(bf16[768,2304]{1,0:T(8,128)(2,1)} %all-gather.9.cloned.1.call-done, f32[1024,768]{0,1:T(8,128)} %copy-done.4, f32[768]{0:T(1024)S(1)} %convert_element_type.164, f32[1024]{0:T(1024)S(1)} %add_rsqrt_fusion, f32[1024]{0:T(1024)S(1)} %broadcast_multiply_fusion.7), kind=kOutput, calls=%fused_computation.187 | convolution fusion | flops 3627024384 | bytes 16133120 | tf_op jit(solution)/shard_map/dot_general | solution.py:207
  225.4 7.5 %all-gather.11.cloned.1.call-done = bf16[1152,768]{1,0:T(8,128)(2,1)} async-done(((bf16[144,768]{1,0:T(8,128)(2,1)}), bf16[1152,768]{1,0:T(8,128)(2,1)}) %all-gather.11.cloned.1.call-update) | async-done | bytes 1769488 | tf_op jit(solution)/shard_map/all_gather | solution.py:190
  232.8 9.2 %fusion.61 = (bf16[1024,1152]{1,0:T(8,128)(2,1)S(1)}, bf16[1024,1152]{1,0:T(8,128)(2,1)S(1)}, bf16[1024,1152]{1,0:T(8,128)(2,1)}) fusion(f32[1024,2304]{1,0:T(8,128)} %fusion.110, bf16[1024,768]{1,0:T(8,128)(2,1)S(1)} %copy-done.20, bf16[1152,768]{1,0:T(8,128)(2,1)} %all-gather.11.cloned.1.call-done), kind=kOutput, calls=%fused_computation.78 | convolution fusion | flops 1830813696 | bytes 19857408 | tf_op jit(solution)/shard_map/td,fd->tf/dot_general | solution.py:227
  242.1 4.9 multiply_reduce_fusion.1
  252.6 5.5 fusion.113
  259.5 4.5 convolution_convert_fusion
  270.5 9.3 %fusion.83 = f32[768,2304]{1,0:T(8,128)} fusion(bf16[1024,1152]{1,0:T(8,128)(2,1)} %copy-done.36, bf16[1024,1152]{1,0:T(8,128)(2,1)} %copy-done.35, f32[1024,768]{0,1:T(8,128)S(1)} %copy-done.6, f32[768]{0:T(1024)S(1)} %convert_element_type.164, f32[1024]{0:T(1024)S(1)} %add_rsqrt_fusion, f32[1024]{0:T(1024)S(1)} %broadcast_multiply_fusion.7), kind=kOutput, calls=%fused_computation.123 | convolution fusion | flops 3636461568 | bytes 14953472 | tf_op jit(solution)/shard_map/td,te->de/dot_general | solution.py:232
  279.8 95.7 %while.31 = (s32[]{:T(128)}, f32[6,512,4,64]{1,3,2,0:T(8,128)}, f32[6,640,4,64]{1,3,2,0:T(8,128)}, f32[6,640,4,64]{1,3,2,0:T(8,128)}, bf16[6,640,4,64]{1,3,2,0:T...) while((s32[]{:T(128)}, f32[6,512,4,64]{1,3,2,0:T(8,128)}, ...), condition=%wide.region_12.13_spmd, body=%wide.region_10.12_spmd.sunk | while | flops 860128896 | bytes 44572060 | solution.py:171
  375.6 5.2 copy.70
  394.9 5.2 copy.71
  406.9 4.3 reshape.527
  411.2 5.6 reshape.526
  420.8 5.6 reshape.532
  426.4 6.0 reshape.531
  432.5 4.1 fusion.86
  445.9 6.2 fusion.94
  452.8 9.3 %fusion.74 = (f32[768]{0:T(1024)S(1)}, f32[1024]{0:T(1024)S(1)}, f32[1024]{0:T(1024)S(1)}, f32[1024,768]{0,1:T(8,128)}) fusion(bf16[1024,768]{0,1:T(8,128)(2,1)S(1)} %copy-done.2, f32[1024]{0:T(1024)S(1)} %copy-done.26, f32[1024]{0:T(1024)S(1)} %copy-done.24, f32[768]{0:T(1024)S(1)} %copy-done.28, bf16[768,2304]{1,0:T(8,128)(2,1)} %all-gather.5.cloned.1.call-done, ...), kind=kOutput, calls=%fused_computation.97 | convolution fusion | flops 3630953728 | bytes 12998656 | tf_op jit(solution)/shard_map/te,de->td/dot_general | solution.py:261
  462.1 20.3 %all-reduce.12 = (bf16[768]{0:T(1024)(128)(2,1)S(1)}, bf16[768]{0:T(1024)(128)(2,1)S(1)}) all-reduce(f32[768]{0:T(1024)S(1)} %get-tuple-element.264, f32[768]{0:T(1024)S(1)} %copy-done.29), channel_id=2, replica_groups=mesh['replica'=4,'shard'=8] {'shard'}, use_global_device_ids=true, to_apply=%region_16.17.clone | all-reduce | flops 1536 | bytes 9216
  482.6 6.2 all-reduce.14
  498.8 36.7 %reduce-scatter.9.cloned.1.call-done = f32[96,2304]{1,0:T(8,128)} async-done(((f32[768,2304]{1,0:T(8,128)}), f32[96,2304]{1,0:T(8,128)}) %reduce-scatter.9.cloned.1.call-update) | async-done | bytes 884752 | tf_op jit(solution)/shard_map/reduce_scatter | solution.py:243
  537.5 130.3 %reduce-scatter.5.cloned.1.call-done = f32[96,2304]{1,0:T(8,128)} async-done(((f32[768,2304]{1,0:T(8,128)}), f32[96,2304]{1,0:T(8,128)}) %reduce-scatter.5.cloned.1.call-update) | async-done | bytes 884752 | tf_op jit(solution)/shard_map/reduce_scatter | solution.py:271
  669.8 5.6 add_convert_fusion
  678.0 31.1 %all-reduce.18.cloned.1.call-done = (bf16[96,2304]{1,0:T(8,128)(2,1)}, bf16[96,768]{1,0:T(8,128)(2,1)}, bf16[96,2304]{1,0:T(8,128)(2,1)}, bf16[144,768]{1,0:T(8,128)(2,1)}) async-done(((bf16[96,2304]{1,0:T(8,128)(2,1)}, bf16[96,768]{1,0:T(8,128)(2,1)}, bf16[96,2304]{1,0:T(8,128)(2,1)}, bf16[144,768]{1,0:T(8,128)(2,1)}), (bf16[96,2304]{1,0:T(8,128)(2,1)}, bf16[96,768]{1,0:T(8,128)(2,1)}, ...) | async-done | bytes 1253392 | tf_op jit(solution)/shard_map/psum | solution.py:276
  (311 shorter events, 279.9 us)
Async XLA Ops:
  7.2 71.2 %all-gather.5.cloned.1.call-start = ((), (), s32[]{:S(2)}) async-start(), calls=%async_computation.4 | async-start | bytes 3981312 | tf_op jit(solution)/shard_map/all_gather | solution.py:184
  7.9 201.3 %all-gather.7.cloned.1.call-start = ((), (), s32[]{:S(2)}) async-start(), calls=%async_computation.5 | async-start | bytes 1327104 | tf_op jit(solution)/shard_map/all_gather | solution.py:185
  8.6 206.0 %all-gather.9.cloned.1.call-start = ((), (), s32[]{:S(2)}) async-start(), calls=%async_computation.6 | async-start | bytes 3981312 | tf_op jit(solution)/shard_map/all_gather | solution.py:189
  9.4 223.4 %all-gather.11.cloned.1.call-start = ((), (), s32[]{:S(2)}) async-start(), calls=%async_computation.7 | async-start | bytes 1990656 | tf_op jit(solution)/shard_map/all_gather | solution.py:190
  10.0 485.3 %reduce-scatter.7.cloned.1.call-start = ((), (), s32[]{:S(2)}) async-start(), calls=%async_computation.9 | async-start | bytes 2654208 | tf_op jit(solution)/shard_map/reduce_scatter | solution.py:272
  10.1 3.9 copy-start.33
  10.1 4.1 copy-start.34
  11.9 197.4 %copy-start.1 = (bf16[1024,768]{0,1:T(8,128)(2,1)}, bf16[1024,768]{0,1:T(8,128)(2,1)S(1)}, u32[]{:S(2)}) copy-start(bf16[1024,768]{0,1:T(8,128)(2,1)S(1)} %copy.59) | copy-start | bytes 4718596
  12.1 66.2 %copy-start.23 = (f32[1024]{0:T(1024)}, f32[1024]{0:T(1024)S(1)}, u32[]{:S(2)}) copy-start(f32[1024]{0:T(1024)S(1)} %broadcast_multiply_fusion.8) | copy-start | bytes 12292
  12.6 71.7 %copy-start.25 = (f32[1024]{0:T(1024)}, f32[1024]{0:T(1024)S(1)}, u32[]{:S(2)}) copy-start(f32[1024]{0:T(1024)S(1)} %add_rsqrt_fusion.1) | copy-start | bytes 12292
  37.9 46.5 %copy-start.27 = (f32[768]{0:T(1024)}, f32[768]{0:T(1024)S(1)}, u32[]{:S(2)}) copy-start(f32[768]{0:T(1024)S(1)} %convert_element_type.157) | copy-start | bytes 9220
  39.0 51.3 %copy-start.16 = (f32[1024,64]{0,1:T(8,128)}, f32[1024,64]{0,1:T(8,128)S(1)}, u32[]{:S(2)}) copy-start(f32[1024,64]{0,1:T(8,128)S(1)} %get-tuple-element.338) | copy-start | bytes 786436
  39.0 51.3 %copy-start.18 = (f32[1024,64]{0,1:T(8,128)}, f32[1024,64]{0,1:T(8,128)S(1)}, u32[]{:S(2)}) copy-start(f32[1024,64]{0,1:T(8,128)S(1)} %get-tuple-element.339) | copy-start | bytes 786436
  100.0 4.1 copy-start.9
  214.7 18.2 %copy-start.20 = (bf16[1024,768]{1,0:T(8,128)(2,1)S(1)}, bf16[1024,768]{1,0:T(8,128)(2,1)}, u32[]{:S(2)}) copy-start(bf16[1024,768]{1,0:T(8,128)(2,1)} %param.19) | copy-start | bytes 4718596
  232.8 9.2 %copy-start.5 = (f32[1024,768]{0,1:T(8,128)S(1)}, f32[1024,768]{0,1:T(8,128)}, u32[]{:S(2)}) copy-start(f32[1024,768]{0,1:T(8,128)} %copy-done.4) | copy-start | bytes 9437188
  232.8 9.2 %copy-start.31 = (bf16[768,2304]{1,0:T(8,128)(2,1)S(1)}, bf16[768,2304]{1,0:T(8,128)(2,1)}, u32[]{:S(2)}) copy-start(bf16[768,2304]{1,0:T(8,128)(2,1)} %all-gather.9.cloned.1.call-done) | copy-start | bytes 10616836
  242.0 4.9 copy-start.35
  242.0 4.9 copy-start.36
  242.1 4.9 copy-start.11
  252.6 244.5 %reduce-scatter.11.cloned.1.call-start = ((), (), s32[]{:S(2)}) async-start(), calls=%async_computation.11 | async-start | bytes 3981312 | tf_op jit(solution)/shard_map/reduce_scatter | solution.py:244
  258.1 277.4 %reduce-scatter.9.cloned.1.call-start = ((), (), s32[]{:S(2)}) async-start(), calls=%async_computation.10 | async-start | bytes 7962624 | tf_op jit(solution)/shard_map/reduce_scatter | solution.py:243
  279.8 388.0 %reduce-scatter.5.cloned.1.call-start = ((), (), s32[]{:S(2)}) async-start(), calls=%async_computation.8 | async-start | bytes 7962624 | tf_op jit(solution)/shard_map/reduce_scatter | solution.py:271
  381.9 2.8 copy-start.14
  401.2 2.8 copy-start.15
  432.5 4.1 copy-start
  432.5 4.5 copy-start.10
  432.5 4.5 copy-start.19
  452.2 256.9 %all-reduce.18.cloned.1.call-start = ((), (), s32[]{:S(2)}) async-start(), calls=%async_computation.12 | async-start | bytes 2506752 | tf_op jit(solution)/shard_map/psum | solution.py:276
  452.8 9.3 %copy-start.29 = (f32[768]{0:T(1024)S(1)}, f32[768]{0:T(1024)}, u32[]{:S(2)}) copy-start(f32[768]{0:T(1024)} %get-tuple-element.262) | copy-start | bytes 9220
  495.3 174.5 %copy-start.7 = (f32[1024,768]{0,1:T(8,128)S(1)}, f32[1024,768]{0,1:T(8,128)}, u32[]{:S(2)}) copy-start(f32[1024,768]{0,1:T(8,128)} %copy-done.4) | copy-start | bytes 9437188
  709.0 5.7 copy-start.22
  (15 other events, 33.8 us)
Sparse Core Ops, SparseCore 0:
  10.2 68.1 all-gather.4
  80.5 39.5 all-gather.6
  122.3 63.9 all-gather.8
  188.3 44.4 all-gather.10
  252.7 68.0 reduce-scatter.6
  324.2 78.1 reduce-scatter.10
  406.1 129.3 reduce-scatter.8
  539.6 128.0 reduce-scatter.4
  671.0 38.0 all-reduce.17
where the time goes:
time: 734 us; the launch traced here: 722 us
  waiting for transfers between devices  240 us (33%)
  matrix products  179 us (24%)
  local copies, waits for them, and re-layouts  142 us (19%)
  other arithmetic  86 us (12%)
  blocking collectives  50 us (7%)
  between operations  16 us (2%)
  loops' own time  8.62 us (1%)
    reduce_scatter x1, waiting for transfers between devices, body(): lax.psum_scatter(attn_members[1], 'shard', scatter_dimension=0, tiled=True)  130 us
    unnamed x2, blocking collectives  43.8 us
    reduce_scatter x1, waiting for transfers between devices, body(): lax.psum_scatter(ffn_members[1], 'shard', scatter_dimension=0, tiled=True)  36.7 us
    all_gather x1, waiting for transfers between devices, body(): lax.all_gather(w_qkv, 'shard', axis=0, tiled=True)  31.9 us
    psum x1, waiting for transfers between devices, body(): lax.psum(owned_qkv.astype(jnp.bfloat16), 'replica').astype(jnp.float32)  31.1 us
    dot_general x12, matrix products, block_scores(): jnp.einsum('qhd,khd->hqk', query_part, key_part, preferred_element_type=j...  24.6 us
    unnamed x86, local copies, waits for them, and re-layouts  21.1 us
    dot_general x6, matrix products, one_block(): jnp.einsum('hqk,khd->qhd', probs, value_part, preferred_element_type=jnp....  20.8 us
  transfers between devices with their start and end apart: 9, of which 5 were waited for; matrix products, arithmetic and copies ran while one was open for 51% of the time, Pallas kernels for 0%

commit v1 on v0

--- a/solution.py
+++ b/solution.py
@@ -11,6 +11,18 @@
 WINDOW = 128
 LENGTH = 1024
 epsilon = 1e-05
+
+
+def collect(value, axis, dim):
+    ways, here = (lax.axis_size(axis), lax.axis_index(axis))
+    grown, reach = (value, 1)
+    while reach < ways:
+        theirs = lax.ppermute(grown, axis, [(d, d ^ reach) for d in range(ways)])
+        mine_first = jnp.concatenate([grown, theirs], axis=dim)
+        theirs_first = jnp.concatenate([theirs, grown], axis=dim)
+        grown = jnp.where(here & reach == 0, mine_first, theirs_first)
+        reach = 2 * reach
+    return grown
 
 
 def normalize(values):
@@ -181,7 +193,7 @@
     count_tok = tokens.shape[0]
     gain_one, joint_weight, out_weight = (
         lax.all_gather(gain_attn, "shard", axis=0, tiled=True),
-        lax.all_gather(w_qkv, "shard", axis=0, tiled=True),
+        collect(w_qkv, "shard", 0),
         lax.all_gather(w_out, "shard", axis=0, tiled=True),
     )
     gain_two, in_weight, down_weight = (

time: 734 us -> 836 us (1.14)
  waiting for transfers between devices: 240 us -> 321 us
  blocking collectives: 50 us -> 67.1 us
    ppermute x0 -> x3, waiting for transfers between devices: none -> 120 us  [collect(): theirs = lax.ppermute(grown, axis, [(d, d ^ reach) for d in range(ways)])]
    all_gather x1, waiting for transfers between devices: 31.9 us -> 0.02 us  [body(): lax.all_gather(w_qkv, 'shard', axis=0, tiled=True)]
    unnamed x2, blocking collectives: 43.8 us -> 60.9 us
  transfers between devices with their start and end apart: 9 -> 12, of which waited for: 5 -> 5; matrix products, arithmetic and copies ran while one was open for 51% -> 47% of each run, Pallas kernels for 0% -> 0%
where the time goes in v1:
time: 836 us; the launch traced here: 824 us
  waiting for transfers between devices  321 us (38%)
  matrix products  177 us (21%)
  local copies, waits for them, and re-layouts  141 us (17%)
  other arithmetic  87.9 us (11%)
  blocking collectives  67.1 us (8%)
  between operations  16.1 us (2%)
  loops' own time  8.62 us (1%)
    reduce_scatter x1, waiting for transfers between devices, body(): lax.psum_scatter(attn_members[1], 'shard', scatter_dimension=0, tiled=True)  130 us
    ppermute x3, waiting for transfers between devices, collect(): theirs = lax.ppermute(grown, axis, [(d, d ^ reach) for d in range(ways)])  120 us
    unnamed x2, blocking collectives  60.9 us
    reduce_scatter x1, waiting for transfers between devices, body(): lax.psum_scatter(ffn_members[1], 'shard', scatter_dimension=0, tiled=True)  37.5 us
    psum x1, waiting for transfers between devices, body(): lax.psum(owned_qkv.astype(jnp.bfloat16), 'replica').astype(jnp.float32)  31.1 us
    dot_general x12, matrix products, block_scores(): jnp.einsum('qhd,khd->hqk', query_part, key_part, preferred_element_type=j...  24.6 us
    unnamed x86, local copies, waits for them, and re-layouts  20.9 us
    dot_general x6, matrix products, one_block(): jnp.einsum('hqk,khd->qhd', probs, value_part, preferred_element_type=jnp....  20.8 us
  transfers between devices with their start and end apart: 12, of which 5 were waited for; matrix products, arithmetic and copies ran while one was open for 47% of the time, Pallas kernels for 0%

profile of v1, /device:TPU:0, one launch (start us, length us, event | category | flops | bytes accessed | tf_op | source)
XLA Modules:
  0.0 823.9 jit_solution(1509550396945749144)
XLA Ops:
  12.5 11.1 %collective-permute-done = bf16[96,2304]{1,0:T(8,128)(2,1)S(1)} collective-permute-done((bf16[96,2304]{1,0:T(8,128)(2,1)}, bf16[96,2304]{1,0:T(8,128)(2,1)S(1)}, u32[]{:S(2)}, u32[]{:S(2)}) %collective-permute-start) | collective-permute-done | bytes 442400 | tf_op jit(solution)/shard_map/ppermute | solution.py:20
  30.1 40.6 %all-reduce.13 = (bf16[768]{0:T(1024)(128)(2,1)S(1)}, bf16[768]{0:T(1024)(128)(2,1)S(1)}) all-reduce(bf16[768]{0:T(1024)(128)(2,1)S(1)} %dynamic-update-slice, bf16[768]{0:T(1024)(128)(2,1)S(1)} %dynamic-update-slice.1), channel_id=1, replica_groups=mesh['replica'=4,'shard'=8] {'shard'}, use_global_device_ids=true, to_apply=%add.8 | all-reduce | flops 1536 | bytes 6144
  75.3 4.4 fusion.107
  80.5 108.6 %collective-permute-done.2 = bf16[384,2304]{1,0:T(8,128)(2,1)S(1)} collective-permute-done((bf16[384,2304]{1,0:T(8,128)(2,1)S(1)}, bf16[384,2304]{1,0:T(8,128)(2,1)S(1)}, u32[]{:S(2)}, u32[]{:S(2)}) %collective-permute-start.2) | collective-permute-done | bytes 1769504 | tf_op jit(solution)/shard_map/ppermute | solution.py:20
  189.1 4.0 fusion.68
  193.1 4.1 slice_bitcast_fusion
  221.7 5.6 squeeze.70
  227.3 4.7 fusion.97
  252.0 61.0 %while.30 = (s32[]{:T(128)}, bf16[6,512,4,64]{1,3,2,0:T(8,128)(2,1)}, f32[6,4,512]{2,1,0:T(4,128)}, bf16[6,640,4,64]{1,3,2,0:T(8,128)(2,1)}, s32[6]{0:T(128)S(1)...) while((s32[]{:T(128)}, ...), condition=%wide.region_5.6_spmd, body=%wide.region_2.5_spmd.sunk | while | flops 352716416 | bytes 18297728 | solution.py:143
  323.1 10.6 %fusion.117 = f32[1024,2304]{1,0:T(8,128)} fusion(bf16[768,2304]{1,0:T(8,128)(2,1)} %all-gather.7.cloned.1.call-done, f32[1024,768]{0,1:T(8,128)} %copy-done.4, f32[768]{0:T(1024)S(1)} %convert_element_type.164, f32[1024]{0:T(1024)S(1)} %add_rsqrt_fusion, f32[1024]{0:T(1024)S(1)} %broadcast_multiply_fusion.7), kind=kOutput, calls=%fused_computation.197 | convolution fusion | flops 3627024384 | bytes 16133120 | tf_op jit(solution)/shard_map/dot_general | solution.py:219
  333.7 9.2 %fusion.61 = (bf16[1024,1152]{1,0:T(8,128)(2,1)S(1)}, bf16[1024,1152]{1,0:T(8,128)(2,1)S(1)}, bf16[1024,1152]{1,0:T(8,128)(2,1)}) fusion(f32[1024,2304]{1,0:T(8,128)} %fusion.117, bf16[1024,768]{1,0:T(8,128)(2,1)S(1)} %copy-done.20, bf16[1152,768]{1,0:T(8,128)(2,1)} %all-gather.9.cloned.1.call-done), kind=kOutput, calls=%fused_computation.78 | convolution fusion | flops 1830813696 | bytes 19857408 | tf_op jit(solution)/shard_map/td,fd->tf/dot_general | solution.py:239
  343.0 4.9 multiply_reduce_fusion.1
  353.5 5.5 fusion.120
  360.4 4.5 convolution_convert_fusion
  371.4 9.3 %fusion.90 = f32[768,2304]{1,0:T(8,128)} fusion(bf16[1024,1152]{1,0:T(8,128)(2,1)} %copy-done.36, bf16[1024,1152]{1,0:T(8,128)(2,1)} %copy-done.35, f32[1024,768]{0,1:T(8,128)S(1)} %copy-done.6, f32[768]{0:T(1024)S(1)} %convert_element_type.164, f32[1024]{0:T(1024)S(1)} %add_rsqrt_fusion, f32[1024]{0:T(1024)S(1)} %broadcast_multiply_fusion.7), kind=kOutput, calls=%fused_computation.131 | convolution fusion | flops 3636461568 | bytes 14953472 | tf_op jit(solution)/shard_map/td,te->de/dot_general | solution.py:244
  380.7 95.8 %while.31 = (s32[]{:T(128)}, f32[6,512,4,64]{1,3,2,0:T(8,128)}, f32[6,640,4,64]{1,3,2,0:T(8,128)}, f32[6,640,4,64]{1,3,2,0:T(8,128)}, bf16[6,640,4,64]{1,3,2,0:T...) while((s32[]{:T(128)}, f32[6,512,4,64]{1,3,2,0:T(8,128)}, ...), condition=%wide.region_12.13_spmd, body=%wide.region_10.12_spmd.sunk | while | flops 860128896 | bytes 44572060 | solution.py:183
  476.5 5.2 copy.70
  495.8 5.2 copy.71
  507.8 4.3 reshape.527
  512.1 5.6 reshape.526
  517.7 4.0 pad.36
  521.7 5.6 reshape.532
  527.3 6.0 reshape.531
  533.4 4.1 fusion.93
  546.8 6.2 fusion.101
  553.8 9.3 %fusion.81 = (f32[768]{0:T(1024)S(1)}, f32[1024]{0:T(1024)S(1)}, f32[1024]{0:T(1024)S(1)}, f32[1024,768]{0,1:T(8,128)}) fusion(bf16[1024,768]{0,1:T(8,128)(2,1)S(1)} %copy-done.2, f32[1024]{0:T(1024)S(1)} %copy-done.28, f32[1024]{0:T(1024)S(1)} %copy-done.24, f32[768]{0:T(1024)S(1)} %copy-done.26, bf16[768,2304]{1,0:T(8,128)(2,1)} %all-gather.11.cloned.1.call-done, ...), kind=kOutput, calls=%fused_computation.105 | convolution fusion | flops 3630953728 | bytes 12998656 | tf_op jit(solution)/shard_map/te,de->td/dot_general | solution.py:273
  563.1 20.2 %all-reduce.12 = (bf16[768]{0:T(1024)(128)(2,1)S(1)}, bf16[768]{0:T(1024)(128)(2,1)S(1)}) all-reduce(f32[768]{0:T(1024)S(1)} %get-tuple-element.264, f32[768]{0:T(1024)S(1)} %copy-done.29), channel_id=2, replica_groups=mesh['replica'=4,'shard'=8] {'shard'}, use_global_device_ids=true, to_apply=%region_16.17.clone | all-reduce | flops 1536 | bytes 9216
  583.5 6.2 all-reduce.14
  599.7 37.5 %reduce-scatter.9.cloned.1.call-done = f32[96,2304]{1,0:T(8,128)} async-done(((f32[768,2304]{1,0:T(8,128)}), f32[96,2304]{1,0:T(8,128)}) %reduce-scatter.9.cloned.1.call-update) | async-done | bytes 884752 | tf_op jit(solution)/shard_map/reduce_scatter | solution.py:255
  639.2 130.3 %reduce-scatter.5.cloned.1.call-done = f32[96,2304]{1,0:T(8,128)} async-done(((f32[768,2304]{1,0:T(8,128)}), f32[96,2304]{1,0:T(8,128)}) %reduce-scatter.5.cloned.1.call-update) | async-done | bytes 884752 | tf_op jit(solution)/shard_map/reduce_scatter | solution.py:283
  771.5 5.6 add_convert_fusion
  779.6 31.1 %all-reduce.18.cloned.1.call-done = (bf16[96,2304]{1,0:T(8,128)(2,1)}, bf16[96,768]{1,0:T(8,128)(2,1)}, bf16[96,2304]{1,0:T(8,128)(2,1)}, bf16[144,768]{1,0:T(8,128)(2,1)}) async-done(((bf16[96,2304]{1,0:T(8,128)(2,1)}, bf16[96,768]{1,0:T(8,128)(2,1)}, bf16[96,2304]{1,0:T(8,128)(2,1)}, bf16[144,768]{1,0:T(8,128)(2,1)}), (bf16[96,2304]{1,0:T(8,128)(2,1)}, bf16[96,768]{1,0:T(8,128)(2,1)}, ...) | async-done | bytes 1253392 | tf_op jit(solution)/shard_map/psum | solution.py:288
  (319 shorter events, 285.7 us)
Async XLA Ops:
  7.2 21.1 %copy-start.30 = (u32[32]{0:T(128)S(1)}, u32[32]{0:T(128)}, u32[]{:S(2)}) copy-start(u32[32]{0:T(128)} %constant.216) | copy-start | bytes 388
  7.2 22.5 %copy-start.33 = (bf16[96]{0:T(256)(128)(2,1)S(1)}, bf16[96]{0:T(256)(128)(2,1)}, u32[]{:S(2)}) copy-start(bf16[96]{0:T(256)(128)(2,1)} %param.13) | copy-start | bytes 580
  7.2 22.7 %copy-start.34 = (bf16[96]{0:T(256)(128)(2,1)S(1)}, bf16[96]{0:T(256)(128)(2,1)}, u32[]{:S(2)}) copy-start(bf16[96]{0:T(256)(128)(2,1)} %param.16) | copy-start | bytes 580
  7.2 310.4 %all-gather.5.cloned.1.call-start = ((), (), s32[]{:S(2)}) async-start(), calls=%async_computation.4 | async-start | bytes 1327104 | tf_op jit(solution)/shard_map/all_gather | solution.py:197
  7.9 315.1 %all-gather.7.cloned.1.call-start = ((), (), s32[]{:S(2)}) async-start(), calls=%async_computation.5 | async-start | bytes 3981312 | tf_op jit(solution)/shard_map/all_gather | solution.py:201
  8.7 325.0 %all-gather.9.cloned.1.call-start = ((), (), s32[]{:S(2)}) async-start(), calls=%async_computation.6 | async-start | bytes 1990656 | tf_op jit(solution)/shard_map/all_gather | solution.py:202
  9.4 544.3 %all-gather.11.cloned.1.call-start = ((), (), s32[]{:S(2)}) async-start(), calls=%async_computation.7 | async-start | bytes 3981312 | tf_op jit(solution)/shard_map/all_gather | solution.py:229
  9.5 14.2 %collective-permute-start = (bf16[96,2304]{1,0:T(8,128)(2,1)}, bf16[96,2304]{1,0:T(8,128)(2,1)S(1)}, u32[]{:S(2)}, u32[]{:S(2)}) collective-permute-start(bf16[96,2304]{1,0:T(8,128)(2,1)} %param.14), channel_id=1, source_target_pairs={{0,1},{1,0},{2,3},{3,2},{4,5},{5,4},{6,7},{7,6},{8,9},{9,8},{10,11... | collective-permute-start | bytes 1327112 | tf_op jit(solution)/shard_map/ppermute | solution.py:20
  25.0 48.5 %collective-permute-start.1 = (bf16[192,2304]{1,0:T(8,128)(2,1)S(1)}, bf16[192,2304]{1,0:T(8,128)(2,1)S(1)}, u32[]{:S(2)}, u32[]{:S(2)}) collective-permute-start(bf16[192,2304]{1,0:T(8,128)(2,1)S(1)} %maximum_select_fusion.3), channel_id=1, source_target_pairs={{0,2},{1,3},{2,0},{3,1},{4,6},{5,7},{6,4},{7,5},{8,10},{9,11},{10,... | collective-permute-start | bytes 2654216 | tf_op jit(solution)/shard_map/ppermute | solution.py:20
  26.4 569.8 %reduce-scatter.7.cloned.1.call-start = ((), (), s32[]{:S(2)}) async-start(), calls=%async_computation.9 | async-start | bytes 2654208 | tf_op jit(solution)/shard_map/reduce_scatter | solution.py:284
  28.2 289.4 %copy-start.1 = (bf16[1024,768]{0,1:T(8,128)(2,1)}, bf16[1024,768]{0,1:T(8,128)(2,1)S(1)}, u32[]{:S(2)}) copy-start(bf16[1024,768]{0,1:T(8,128)(2,1)S(1)} %copy.59) | copy-start | bytes 4718596
  70.7 118.4 %copy-start.25 = (f32[768]{0:T(1024)}, f32[768]{0:T(1024)S(1)}, u32[]{:S(2)}) copy-start(f32[768]{0:T(1024)S(1)} %convert_element_type.157) | copy-start | bytes 9220
  74.0 115.0 %collective-permute-start.2 = (bf16[384,2304]{1,0:T(8,128)(2,1)S(1)}, bf16[384,2304]{1,0:T(8,128)(2,1)S(1)}, u32[]{:S(2)}, u32[]{:S(2)}) collective-permute-start(bf16[384,2304]{1,0:T(8,128)(2,1)S(1)} %maximum_select_fusion.2), channel_id=1, source_target_pairs={{0,4},{1,5},{2,6},{3,7},{4,0},{5,1},{6,2},{7,3},{8,12},{9,13},{10,... | collective-permute-start | bytes 5308424 | tf_op jit(solution)/shard_map/ppermute | solution.py:20
  75.2 123.7 %copy-start.16 = (f32[1024,64]{0,1:T(8,128)}, f32[1024,64]{0,1:T(8,128)S(1)}, u32[]{:S(2)}) copy-start(f32[1024,64]{0,1:T(8,128)S(1)} %get-tuple-element.338) | copy-start | bytes 786436
  75.2 123.7 %copy-start.18 = (f32[1024,64]{0,1:T(8,128)}, f32[1024,64]{0,1:T(8,128)S(1)}, u32[]{:S(2)}) copy-start(f32[1024,64]{0,1:T(8,128)S(1)} %get-tuple-element.339) | copy-start | bytes 786436
  80.0 113.1 %copy-start.23 = (f32[1024]{0:T(1024)}, f32[1024]{0:T(1024)S(1)}, u32[]{:S(2)}) copy-start(f32[1024]{0:T(1024)S(1)} %broadcast_multiply_fusion.8) | copy-start | bytes 12292
  80.5 112.6 %copy-start.27 = (f32[1024]{0:T(1024)}, f32[1024]{0:T(1024)S(1)}, u32[]{:S(2)}) copy-start(f32[1024]{0:T(1024)S(1)} %add_rsqrt_fusion.1) | copy-start | bytes 12292
  323.0 10.7 %copy-start.20 = (bf16[1024,768]{1,0:T(8,128)(2,1)S(1)}, bf16[1024,768]{1,0:T(8,128)(2,1)}, u32[]{:S(2)}) copy-start(bf16[1024,768]{1,0:T(8,128)(2,1)} %param.19) | copy-start | bytes 4718596
  333.7 9.2 %copy-start.5 = (f32[1024,768]{0,1:T(8,128)S(1)}, f32[1024,768]{0,1:T(8,128)}, u32[]{:S(2)}) copy-start(f32[1024,768]{0,1:T(8,128)} %copy-done.4) | copy-start | bytes 9437188
  333.7 9.2 %copy-start.31 = (bf16[768,2304]{1,0:T(8,128)(2,1)S(1)}, bf16[768,2304]{1,0:T(8,128)(2,1)}, u32[]{:S(2)}) copy-start(bf16[768,2304]{1,0:T(8,128)(2,1)} %all-gather.7.cloned.1.call-done) | copy-start | bytes 10616836
  342.9 4.9 copy-start.35
  342.9 4.9 copy-start.36
  343.0 4.9 copy-start.11
  353.5 244.4 %reduce-scatter.11.cloned.1.call-start = ((), (), s32[]{:S(2)}) async-start(), calls=%async_computation.11 | async-start | bytes 3981312 | tf_op jit(solution)/shard_map/reduce_scatter | solution.py:256
  359.0 278.2 %reduce-scatter.9.cloned.1.call-start = ((), (), s32[]{:S(2)}) async-start(), calls=%async_computation.10 | async-start | bytes 7962624 | tf_op jit(solution)/shard_map/reduce_scatter | solution.py:255
  380.7 388.8 %reduce-scatter.5.cloned.1.call-start = ((), (), s32[]{:S(2)}) async-start(), calls=%async_computation.8 | async-start | bytes 7962624 | tf_op jit(solution)/shard_map/reduce_scatter | solution.py:283
  533.4 4.5 copy-start.10
  533.4 4.5 copy-start.19
  553.0 257.7 %all-reduce.18.cloned.1.call-start = ((), (), s32[]{:S(2)}) async-start(), calls=%async_computation.12 | async-start | bytes 2506752 | tf_op jit(solution)/shard_map/psum | solution.py:288
  553.7 9.3 %copy-start.29 = (f32[768]{0:T(1024)S(1)}, f32[768]{0:T(1024)}, u32[]{:S(2)}) copy-start(f32[768]{0:T(1024)} %get-tuple-element.262) | copy-start | bytes 9220
  596.1 175.3 %copy-start.7 = (f32[1024,768]{0,1:T(8,128)S(1)}, f32[1024,768]{0,1:T(8,128)}, u32[]{:S(2)}) copy-start(f32[1024,768]{0,1:T(8,128)} %copy-done.4) | copy-start | bytes 9437188
  810.7 5.7 copy-start.22
  (18 other events, 45.1 us)
Sparse Core Ops, SparseCore 0:
  10.2 49.0 all-gather.4
  61.5 119.7 all-gather.6
  183.6 44.8 all-gather.8
  230.5 64.1 all-gather.10
  353.6 67.9 reduce-scatter.6
  425.1 78.2 reduce-scatter.10
  507.1 130.1 reduce-scatter.8
  641.3 128.0 reduce-scatter.4
  772.7 38.0 all-reduce.17
